TPU v7x, 32 devices: a whole 2x2x4 slice. The times are simulated.
32 devices in a mesh: px: 8 (over y, x, core), py: 4 (over z).
Axes of the slice: x: 2, y: 2, z: 4, core: 2. Of those that a mesh axis runs over, the one named last changes fastest.
Arguments:
- displacement: float32 [60, 16, 8, 128], P(None, 'px', 'py'), may hold values from -4 to 4
- velocity: float32 [60, 16, 8, 128], P(None, 'px', 'py'), may hold values from -6 to 6
- modulus: float32 [16, 8, 128], P('px', 'py'), may hold values from 0.5 to 4
- gradient_map: float32 [243, 60], replicated, may hold values from -0.75 to 0.75
- trace_map: float32 [6, 54, 60], replicated, may hold values from -0.75 to 0.75
- lift_map: float32 [6, 60, 54], replicated, may hold values from -0.3125 to 0.3125
- split_map: float32 [27, 27], replicated, may hold values from -1.25 to 1.25
- spread_map: float32 [6, 60, 27], replicated, may hold values from -1.25 to 1.25
- fracture_faces: int32 [32, 512], P(('px', 'py')), may hold values from 0 to 1534, as said below
- fracture_counts: int32 [32, 3], P(('px', 'py')), may hold values from 0 to 256, as said below
Outputs:
- displacement_out: float32 [60, 16, 8, 128], P(None, 'px', 'py')
- velocity_out: float32 [60, 16, 8, 128], P(None, 'px', 'py')
Inputs may be any that keep to these rules, and one draw needn't show every extreme that they name: `fracture_faces`: row p holds the device at index p of px+py (px major). With local element numbers (i * 2 + j) * 128 + k and face ids d * 2 * 2 * 128 + element, slots 0 to 127 name +x faces of elements with i = 1, the next 128 slots +y faces of elements with j = 1, the last 256 slots faces whose neighbour lies on the same device. All ids of a row differ. Only the first fracture_counts[p, s] slots of section s open. `fracture_counts`: counts of opened slots in the three sections of a row. The first is 0 on devices with the last px index, the second on devices with the last py index; over all devices the sections reach 128, 128 and 256.
All inputs are finite; a program needn't handle non-finite values.
Results may differ from a plain program's by a relative error of at most 0.0003.
Values sent between devices are 32-bit elements; how exact they have to be, the bound alone decides.
A program may use at most 64 MiB of HBM per device.

v0:
```python
import jax
import jax.numpy as jnp
from jax import lax
from jax.experimental import pallas as pl
from jax.experimental.pallas import tpu as pltpu
from jax.sharding import PartitionSpec as P

BLK_CAP = 128
penalty = 2.0
damping = 0.5
substep = 0.1
F32 = jnp.float32
BF16 = jnp.bfloat16
MESH = pl.DeviceIdType.MESH


def halves(value):
    high = value.astype(BF16)
    return high, (value - high.astype(F32)).astype(BF16)


def mm(a, b):
    return jnp.dot(a, b, preferred_element_type=F32)


def kernel(
    disp_in, vel_in, mod_in, grad_in, trace_in, lift_in, split_in, spread_in, faces_in, counts_in,
    out_u, out_w, out_f,
    disp, vel, mod, grad, trace, lift, split, spread, faces, counts,
    state, state_b, wa_h, wa_l, lb_h, lb_hl, ew_hl, tp, gp, lp, pp, qp, proj,
    early_h, early_l, late_h, late_l, jump_h, jump_l, send, recv, in_sem, send_sem, recv_sem,
):
    px, py = lax.axis_index("px"), lax.axis_index("py")
    nx, ny = lax.axis_size("px"), lax.axis_size("py")
    there = (px > 0, px < nx - 1, py > 0, py < ny - 1)
    beside = ({"px": px - 1}, {"px": px + 1}, {"py": py - 1}, {"py": py + 1})
    barrier = pltpu.get_barrier_semaphore()
    for side in (2, 3, 0, 1):

        @pl.when(there[side])
        def _(side=side):
            pl.semaphore_signal(barrier, inc=1, device_id=beside[side], device_id_type=MESH)

    names = ("trace", "disp", "vel", "grad", "lift", "mod", "spread", "split", "faces", "counts")
    given = (trace_in, disp_in, vel_in, grad_in, lift_in, mod_in, spread_in, split_in, faces_in, counts_in)
    local = (trace, disp, vel, grad, lift, mod, spread, split, faces, counts)
    loads = {}
    for n, name in enumerate(names):
        loads[name] = pltpu.make_async_copy(given[n], local[n], in_sem.at[n])
        loads[name].start()

    for ref in (state, tp, lp, pp, qp, gp):
        ref[...] = jnp.zeros_like(ref)
    for ref in (late_h, late_l, jump_h, jump_l):
        for d in range(ref.shape[0] // 128):
            ref[128 * d + 112 : 128 * d + 128, :] = jnp.zeros((16, 512), BF16)
    for ref in (early_h, early_l):
        ref[112:128, :] = jnp.zeros((16, 512), BF16)
    for slot, side in ((0, 1), (1, 0), (2, 3), (3, 2)):

        @pl.when(jnp.logical_not(there[side]))
        def _(slot=slot):
            for s in range(3):
                recv[s, slot] = jnp.zeros((56, 256), F32)

    def put_a(row, value):
        high, low = halves(value)
        rows = slice(row, row + value.shape[0])
        wa_h[rows, 0:128] = high
        wa_h[rows, 128:256] = high
        wa_l[rows, :] = low

    row_id = lax.broadcasted_iota(jnp.int32, (56, 128), 0)

    def face_rows(f, sign):
        both = tp[f]
        upper = penalty * both + (sign * 0.5) * pltpu.roll(both, 29, 0)
        upper = upper + pltpu.roll(damping * both, 64, 1)
        lower = jnp.where(row_id < 54, pltpu.roll(both, 27, 0), 0.0)
        return jnp.where(row_id < 27, upper, lower)

    def put_faces(row, d, sign):
        pair = [face_rows(2 * d, sign), face_rows(2 * d + 1, sign)]
        put_a(row + 112 * d, jnp.concatenate(pair, axis=0))

    loads["trace"].wait()
    for f in range(6):
        tp[f, 0:54, 0:60] = trace[f]
    put_faces(0, 0, 1.0)
    put_faces(0, 1, 1.0)

    def block(k):
        return slice(128 * k, 128 * k + 128)

    loads["disp"].wait()
    loads["vel"].wait()
    for k in range(4):
        state[0:60, block(k)] = disp[pl.ds(k, 60, stride=4), :]
        state[64:124, block(k)] = vel[pl.ds(k, 60, stride=4), :]

    copies = [
        [
            pltpu.make_async_remote_copy(
                src_ref=send.at[s, side],
                dst_ref=recv.at[s, side],
                send_sem=send_sem.at[s, side],
                recv_sem=recv_sem.at[s, side],
                device_id=beside[side],
                device_id_type=MESH,
            )
            for side in range(4)
        ]
        for s in range(3)
    ]
    outer = ((0, 1), (2, 3), (0, 2), (1, 3))

    def project_outer(s, open_mask=None):
        for k in range(4):
            high, low = halves(state[:, block(k)])
            state_b[0:128, block(k)] = high
            state_b[128:256, block(k)] = low
        for d in (1, 0):
            rows = slice(112 * d, 112 * d + 112)
            proj[rows, :] = mm(wa_h[rows, :], state_b[...]) + mm(wa_l[rows, :], state_b[0:128, :])
            for f in (2 * d, 2 * d + 1):
                for half in range(2):
                    k = outer[f][half]
                    send[s, f, :, block(half)] = proj[56 * f : 56 * f + 56, block(k)]
                    if s == 2 and f % 2 == 1:
                        row = 4 * d + k
                        send[s, f, 54:55, block(half)] = open_mask[row : row + 1, :]
            if s == 0 and d == 1:
                pl.semaphore_wait(barrier, sum(t.astype(jnp.int32) for t in there))
            for side in (2 * d, 2 * d + 1):

                @pl.when(there[side])
                def _(side=side):
                    copies[s][side].start()

    project_outer(0)

    put_faces(0, 2, 1.0)
    for d in range(3):
        put_faces(336, d, -1.0)
    loads["grad"].wait()
    gp[0:60, 0:243] = grad[...]
    put_a(672, jnp.transpose(gp[...]))

    def put_b(column, value):
        high, low = halves(value)
        columns = slice(column, column + value.shape[1])
        lb_h[:, columns] = high
        lb_hl[0:64, columns] = high
        lb_hl[64:128, columns] = low

    put_b(384, -gp[0:64, :])
    loads["lift"].wait()
    lift_row = lax.broadcasted_iota(jnp.int32, (54, 60), 0)
    for f in range(6):
        at = 56 * (f % 2)
        lp[f // 2, at : at + 54, 0:60] = jnp.where(lift_row < 27, lift[f], 0.5 * lift[f])
    for d in range(3):
        put_b(128 * d, jnp.transpose(lp[d])[0:64, :])

    loads["spread"].wait()
    loads["split"].wait()
    qp[0:27, 0:27] = split[...]
    qp[32:59, 0:27] = split[...]
    row128 = lax.broadcasted_iota(jnp.int32, (128, 128), 0)
    placed = jnp.where(row128 < 32, pltpu.roll(qp[...], 27, 1), pltpu.roll(qp[...], 83, 1))
    for f in range(6):
        at = 32 * (f % 2)
        pp[f // 2, at : at + 27, 0:60] = spread[f]
    for d in range(3):
        part = jnp.dot(
            jnp.transpose(pp[d])[0:64, :],
            placed,
            precision=lax.Precision.HIGHEST,
            preferred_element_type=F32,
        )
        high, low = halves(-part)
        ew_hl[0:64, block(d)] = high
        ew_hl[64:128, block(d)] = low

    loads["faces"].wait()
    loads["counts"].wait()
    loads["mod"].wait()
    ids = faces[...]
    slots = lax.broadcasted_iota(jnp.int32, ids.shape, 1)
    section = jnp.where(slots < BLK_CAP, 0, jnp.where(slots < 2 * BLK_CAP, 1, 2))
    limit = jnp.where(
        section == 0,
        counts[0:1, 0:1],
        jnp.where(section == 1, BLK_CAP + counts[0:1, 1:2], 2 * BLK_CAP + counts[0:1, 2:3]),
    )
    group = jnp.where(slots < limit, ids >> 7, -1)
    spot = ids & 127
    high_hot = lax.broadcasted_iota(jnp.int32, (16, ids.shape[1]), 0) == group
    low_hot = lax.broadcasted_iota(jnp.int32, (128, ids.shape[1]), 0) == spot
    open_mask = lax.dot_general(
        high_hot.astype(F32).astype(BF16),
        low_hot.astype(F32).astype(BF16),
        (((1,), (1,)), ((), ())),
        preferred_element_type=F32,
    )

    alive = [jnp.where(t, 1.0, 0.0).astype(F32) for t in there]
    lane_row = lax.broadcasted_iota(jnp.int32, (1, 128), 1)
    not_first = (lane_row > 0).astype(F32)
    not_last = (lane_row < 127).astype(F32)

    def put(high_ref, low_ref, row, k, value):
        high, low = halves(value)
        rows = slice(row, row + value.shape[0])
        high_ref[rows, block(k)] = high
        low_ref[rows, block(k)] = low

    def traced(f, k):
        return proj[56 * f : 56 * f + 56, block(k)]

    def own(f, k):
        return proj[336 + 56 * f : 392 + 56 * f, block(k)]

    for s in range(3):
        if s > 0:
            project_outer(s, open_mask)
        proj[224:928, :] = mm(wa_h[224:928, :], state_b[...]) + mm(
            wa_l[224:928, :], state_b[0:128, :]
        )
        for k in range(4):
            before = (pltpu.roll(traced(5, k), 1, 1) - own(4, k)) * not_first
            after = (pltpu.roll(traced(4, k), 127, 1) - own(5, k)) * not_last
            put(early_h, early_l, 0, k, jnp.concatenate([before, after], axis=0))
            if s == 2:
                opens = open_mask[8 + k : 9 + k, :]
                pair = [before * pltpu.roll(opens, 1, 1), after * opens]
                put(jump_h, jump_l, 256, k, jnp.concatenate(pair, axis=0))
            put(early_h, early_l, 128, k, proj[672:928, block(k)] * mod[k : k + 1, :])
        both = mm(lb_hl[:, 256:640], early_h[...])
        force = both[0:64] + both[64:128] + mm(lb_h[:, 256:640], early_l[...])

        for d in (0, 1):
            for side in (2 * d, 2 * d + 1):

                @pl.when(there[side])
                def _(s=s, side=side):
                    copies[s][side ^ 1].wait_recv()

            for k in range(4):
                i, j = k // 2, k % 2
                n = k ^ (2 if d == 0 else 1)
                half = j if d == 0 else i
                flux, jump = [], []
                for f in (2 * d, 2 * d + 1):
                    inner = (i, 1 - i, j, 1 - j)[f] == 1
                    if inner:
                        part = traced(f ^ 1, n) - own(f, k)
                    else:
                        part = (recv[s, f ^ 1, :, block(half)] - own(f, k)) * alive[f]
                    flux.append(part)
                    if s == 2:
                        if f % 2:
                            opens = open_mask[4 * d + k : 4 * d + k + 1, :]
                        elif inner:
                            opens = open_mask[4 * d + n : 4 * d + n + 1, :]
                        else:
                            opens = recv[s, f ^ 1, 54:55, block(half)]
                        jump.append(part * opens)
                put(late_h, late_l, 128 * d, k, jnp.concatenate(flux, axis=0))
                if s == 2:
                    put(jump_h, jump_l, 128 * d, k, jnp.concatenate(jump, axis=0))
        both = mm(lb_hl[:, 0:256], late_h[...])
        force = force + both[0:64] + both[64:128] + mm(lb_h[:, 0:256], late_l[...])
        if s < 2:
            velocity = state[64:128, :] + substep * force
            state[64:128, :] = velocity
            state[0:64, :] = state[0:64, :] + substep * velocity
        else:
            both = mm(ew_hl[...], jump_h[...])
            displace = state[0:64, :] + both[0:64] + both[64:128] + mm(ew_hl[0:64, :], jump_l[...])
            for k in range(4):
                out_u[pl.ds(k, 60, stride=4), :] = displace[0:60, block(k)]
                out_w[pl.ds(k, 60, stride=4), :] = state[64:124, block(k)]
                out_f[pl.ds(k, 60, stride=4), :] = force[0:60, block(k)]

    for s in range(3):
        for side in range(4):

            @pl.when(there[side])
            def _(s=s, side=side):
                copies[s][side].wait_send()


def shards(
    displacement, velocity, modulus, gradient_map, trace_map, lift_map, split_map, spread_map,
    fracture_faces, fracture_counts,
):
    shape = displacement.shape
    flat = (shape[0] * 4, 128)
    args = (
        displacement.reshape(flat),
        velocity.reshape(flat),
        modulus.reshape(4, 128),
        gradient_map.T,
        trace_map,
        jnp.transpose(lift_map, (0, 2, 1)),
        split_map,
        jnp.transpose(spread_map, (0, 2, 1)),
        fracture_faces,
        fracture_counts,
    )
    vmem = pl.BlockSpec(memory_space=pltpu.VMEM)
    hbm = pl.BlockSpec(memory_space=pltpu.HBM)
    out = jax.ShapeDtypeStruct(flat, F32)
    opened, velocity_now, force = pl.pallas_call(
        kernel,
        out_shape=(out, out, out),
        in_specs=[hbm] * 10,
        out_specs=(vmem, vmem, vmem),
        scratch_shapes=[
            *(pltpu.VMEM(a.shape, a.dtype) for a in args),
            pltpu.VMEM((128, 512), F32),
            pltpu.VMEM((256, 512), BF16),
            pltpu.VMEM((928, 256), BF16),
            pltpu.VMEM((928, 128), BF16),
            pltpu.VMEM((64, 640), BF16),
            pltpu.VMEM((128, 640), BF16),
            pltpu.VMEM((128, 384), BF16),
            pltpu.VMEM((6, 56, 128), F32),
            pltpu.VMEM((128, 256), F32),
            pltpu.VMEM((3, 128, 128), F32),
            pltpu.VMEM((3, 128, 128), F32),
            pltpu.VMEM((128, 128), F32),
            pltpu.VMEM((928, 512), F32),
            pltpu.VMEM((384, 512), BF16),
            pltpu.VMEM((384, 512), BF16),
            pltpu.VMEM((256, 512), BF16),
            pltpu.VMEM((256, 512), BF16),
            pltpu.VMEM((384, 512), BF16),
            pltpu.VMEM((384, 512), BF16),
            pltpu.VMEM((3, 4, 56, 256), F32),
            pltpu.VMEM((3, 4, 56, 256), F32),
            pltpu.SemaphoreType.DMA((10,)),
            pltpu.SemaphoreType.DMA((3, 4)),
            pltpu.SemaphoreType.DMA((3, 4)),
        ],
        compiler_params=pltpu.CompilerParams(
            collective_id=0, has_side_effects=True, vmem_limit_bytes=40 * 1024 * 1024
        ),
    )(*(pltpu.with_memory_space_constraint(a, pltpu.HBM) for a in args))
    velocity_out = velocity_now + substep * force
    displacement_out = opened + substep * velocity_out
    return displacement_out.reshape(shape), velocity_out.reshape(shape)


def solution(mesh):
    return jax.shard_map(
        shards,
        mesh=mesh,
        in_specs=(
            P(None, "px", "py", None),
            P(None, "px", "py", None),
            P("px", "py", None),
            P(),
            P(),
            P(),
            P(),
            P(),
            P(("px", "py"), None),
            P(("px", "py"), None),
        ),
        out_specs=(P(None, "px", "py", None), P(None, "px", "py", None)),
        check_vma=False,
    )
```

profile of v0, /device:TPU:0, one launch (start us, length us, event | category | flops | bytes accessed | tf_op | source)
XLA Modules:
  0.0 17.5 jit_solution(7192000401398892591)
XLA Ops:
  0.6 16.1 %shard_map.113 = (f32[240,128]{1,0:T(8,128)S(1)}, f32[240,128]{1,0:T(8,128)S(1)}, f32[240,128]{1,0:T(8,128)S(1)}) custom-call(f32[240,128]{1,0:T(8,128)} %bitcast.11, f32[240,128]{1,0:T(8,128)} %bitcast.12, f32[4,128]{1,0:T(4,128)} %bitcast.15, f32[60,243]{1,0:T(8,128)} %bitcast.14, f32[6,54,60]{2,1,0:T(8,128)} %trace_in.1, f32[6,54,60]{2,1,0:T(8,128)} %bitcast.8, ...), custom_call_target="tpu_custom_call" | custom-call | tf_op jit(solution)/shard_map/pallas_call | solution.py:315
  16.8 0.7 %multiply_add_fusion = (f32[240,128]{1,0:T(8,128)}, f32[240,128]{1,0:T(8,128)}) fusion(f32[240,128]{1,0:T(8,128)S(1)} %get-tuple-element.5, f32[240,128]{1,0:T(8,128)S(1)} %get-tuple-element.6, f32[240,128]{1,0:T(8,128)S(1)} %get-tuple-element.7), kind=kLoop, calls=%fused_computation | loop fusion | flops 122880 | bytes 614400 | tf_op jit(solution)/shard_map/add | solution.py:352
where the time goes:
time: 17.7 us; the launch traced here: 17.5 us
  Pallas kernels  16.1 us (91%)
  other arithmetic  0.72 us (4%)
  between operations  0.64 us (4%)
    pallas_call x1, Pallas kernels, shards(): pl.pallas_call(kernel, out_shape=(out, out, out), in_specs=[hbm] * 10, ou...  16.1 us
    add x1, other arithmetic, shards(): displacement_out = opened + substep * velocity_out  0.72 us

commit v1 on v0

--- a/solution.py
+++ b/solution.py
@@ -27,8 +27,9 @@
     disp_in, vel_in, mod_in, grad_in, trace_in, lift_in, split_in, spread_in, faces_in, counts_in,
     out_u, out_w, out_f,
     disp, vel, mod, grad, trace, lift, split, spread, faces, counts,
-    state, state_b, wa_h, wa_l, lb_h, lb_hl, ew_hl, tp, gp, lp, pp, qp, proj,
-    early_h, early_l, late_h, late_l, jump_h, jump_l, send, recv, in_sem, send_sem, recv_sem,
+    state, state_b, wa_h, wa_l, lb_h, lb_hl, ew_hl, cb, tp, gp, lp, pp, qp, proj,
+    own_h, own_l, late_h, late_l, jump_h, jump_l, leap_h, leap_l,
+    send, recv, in_sem, send_sem, recv_sem,
 ):
     px, py = lax.axis_index("px"), lax.axis_index("py")
     nx, ny = lax.axis_size("px"), lax.axis_size("py")
@@ -51,11 +52,6 @@
 
     for ref in (state, tp, lp, pp, qp, gp):
         ref[...] = jnp.zeros_like(ref)
-    for ref in (late_h, late_l, jump_h, jump_l):
-        for d in range(ref.shape[0] // 128):
-            ref[128 * d + 112 : 128 * d + 128, :] = jnp.zeros((16, 512), BF16)
-    for ref in (early_h, early_l):
-        ref[112:128, :] = jnp.zeros((16, 512), BF16)
     for slot, side in ((0, 1), (1, 0), (2, 3), (3, 2)):
 
         @pl.when(jnp.logical_not(there[side]))
@@ -114,31 +110,35 @@
     ]
     outer = ((0, 1), (2, 3), (0, 2), (1, 3))
 
-    def project_outer(s, open_mask=None):
+    def split_state():
         for k in range(4):
             high, low = halves(state[:, block(k)])
             state_b[0:128, block(k)] = high
             state_b[128:256, block(k)] = low
-        for d in (1, 0):
-            rows = slice(112 * d, 112 * d + 112)
-            proj[rows, :] = mm(wa_h[rows, :], state_b[...]) + mm(wa_l[rows, :], state_b[0:128, :])
-            for f in (2 * d, 2 * d + 1):
-                for half in range(2):
-                    k = outer[f][half]
-                    send[s, f, :, block(half)] = proj[56 * f : 56 * f + 56, block(k)]
-                    if s == 2 and f % 2 == 1:
-                        row = 4 * d + k
-                        send[s, f, 54:55, block(half)] = open_mask[row : row + 1, :]
-            if s == 0 and d == 1:
-                pl.semaphore_wait(barrier, sum(t.astype(jnp.int32) for t in there))
-            for side in (2 * d, 2 * d + 1):
-
-                @pl.when(there[side])
-                def _(side=side):
-                    copies[s][side].start()
-
-    project_outer(0)
-
+
+    def project(rows):
+        return mm(wa_h[rows, :], state_b[...]) + mm(wa_l[rows, :], state_b[0:128, :])
+
+    def begin(s, d):
+        for side in (2 * d, 2 * d + 1):
+
+            @pl.when(there[side])
+            def _(side=side):
+                copies[s][side].start()
+
+    split_state()
+    for d in (1, 0):
+        rows = slice(112 * d, 112 * d + 112)
+        proj[rows, :] = project(rows)
+        for f in (2 * d, 2 * d + 1):
+            for half in range(2):
+                send[0, f, :, block(half)] = proj[56 * f : 56 * f + 56, block(outer[f][half])]
+        if d == 1:
+            pl.semaphore_wait(barrier, sum(t.astype(jnp.int32) for t in there))
+        begin(0, d)
+
+    for ref in (late_h, late_l, leap_h, leap_l):
+        ref[...] = jnp.zeros_like(ref)
     put_faces(0, 2, 1.0)
     for d in range(3):
         put_faces(336, d, -1.0)
@@ -157,17 +157,27 @@
     loads["lift"].wait()
     lift_row = lax.broadcasted_iota(jnp.int32, (54, 60), 0)
     for f in range(6):
-        at = 56 * (f % 2)
+        at = 64 * (f % 2)
         lp[f // 2, at : at + 54, 0:60] = jnp.where(lift_row < 27, lift[f], 0.5 * lift[f])
     for d in range(3):
         put_b(128 * d, jnp.transpose(lp[d])[0:64, :])
+
+    reach = []
+    for f in range(4):
+        rows = face_rows(f, 1.0)
+        reach.append((substep * substep) * rows + substep * pltpu.roll(rows, 64, 1))
+    high, low = halves(jnp.concatenate(reach, axis=0)[:, 0:64])
+    carry = mm(high, lb_h[:, 0:256]) + mm(low, lb_h[:, 0:256]) + mm(high, lb_hl[64:128, 0:256])
+    for i in range(2):
+        pieces = [carry[112:224], carry[56 * i : 56 * i + 56], jnp.zeros((8, 256), F32)]
+        cb[i] = jnp.concatenate(pieces, axis=0).astype(BF16)
 
     loads["spread"].wait()
     loads["split"].wait()
     qp[0:27, 0:27] = split[...]
     qp[32:59, 0:27] = split[...]
     row128 = lax.broadcasted_iota(jnp.int32, (128, 128), 0)
-    placed = jnp.where(row128 < 32, pltpu.roll(qp[...], 27, 1), pltpu.roll(qp[...], 83, 1))
+    placed = jnp.where(row128 < 32, pltpu.roll(qp[...], 27, 1), pltpu.roll(qp[...], 91, 1))
     for f in range(6):
         at = 32 * (f % 2)
         pp[f // 2, at : at + 27, 0:60] = spread[f]
@@ -209,6 +219,8 @@
     not_first = (lane_row > 0).astype(F32)
     not_last = (lane_row < 127).astype(F32)
 
+    gap = jnp.zeros((8, 128), F32)
+
     def put(high_ref, low_ref, row, k, value):
         high, low = halves(value)
         rows = slice(row, row + value.shape[0])
@@ -221,66 +233,114 @@
     def own(f, k):
         return proj[336 + 56 * f : 392 + 56 * f, block(k)]
 
+    def came(s, f, half):
+        return jnp.concatenate([recv[s, f ^ 1, :, block(half)], gap], axis=0)
+
+    def mm3(both_ref, high_ref, columns, b_high, b_low):
+        both = mm(both_ref[:, columns], b_high[...])
+        return both[0:64] + both[64:128] + mm(high_ref[:, columns], b_low[...])
+
+    early, lateral = slice(0, 640), slice(0, 256)
     for s in range(3):
         if s > 0:
-            project_outer(s, open_mask)
-        proj[224:928, :] = mm(wa_h[224:928, :], state_b[...]) + mm(
-            wa_l[224:928, :], state_b[0:128, :]
-        )
+            for f in range(4):
+                for half in range(2):
+                    k = outer[f][half]
+                    rest = came(s - 1, f, half) - late_h[64 * f : 64 * f + 64, block(k)].astype(F32)
+                    late_l[64 * f : 64 * f + 64, block(k)] = rest.astype(BF16)
+            force = mm3(lb_hl, lb_h, lateral, late_h, late_l)
+            state[64:128, :] = state[64:128, :] + substep * force
+            state[0:64, :] = state[0:64, :] + (substep * substep) * force
+            split_state()
+        todo = slice(224 if s == 0 else 0, 928)
+        proj[todo, :] = project(todo)
         for k in range(4):
-            before = (pltpu.roll(traced(5, k), 1, 1) - own(4, k)) * not_first
-            after = (pltpu.roll(traced(4, k), 127, 1) - own(5, k)) * not_last
-            put(early_h, early_l, 0, k, jnp.concatenate([before, after], axis=0))
-            if s == 2:
-                opens = open_mask[8 + k : 9 + k, :]
-                pair = [before * pltpu.roll(opens, 1, 1), after * opens]
-                put(jump_h, jump_l, 256, k, jnp.concatenate(pair, axis=0))
-            put(early_h, early_l, 128, k, proj[672:928, block(k)] * mod[k : k + 1, :])
-        both = mm(lb_hl[:, 256:640], early_h[...])
-        force = both[0:64] + both[64:128] + mm(lb_h[:, 256:640], early_l[...])
-
-        for d in (0, 1):
-            for side in (2 * d, 2 * d + 1):
-
-                @pl.when(there[side])
-                def _(s=s, side=side):
-                    copies[s][side ^ 1].wait_recv()
-
-            for k in range(4):
-                i, j = k // 2, k % 2
-                n = k ^ (2 if d == 0 else 1)
-                half = j if d == 0 else i
-                flux, jump = [], []
+            i, j = k // 2, k % 2
+            for d in range(3):
+                n = k if d == 2 else k ^ (2 - d)
+                part, jump = [], []
                 for f in (2 * d, 2 * d + 1):
-                    inner = (i, 1 - i, j, 1 - j)[f] == 1
-                    if inner:
-                        part = traced(f ^ 1, n) - own(f, k)
+                    inner = d == 2 or (i, 1 - i, j, 1 - j)[f] == 1
+                    if f == 4:
+                        now = (pltpu.roll(traced(5, k), 1, 1) - own(4, k)) * not_first
+                    elif f == 5:
+                        now = (pltpu.roll(traced(4, k), 127, 1) - own(5, k)) * not_last
+                    elif inner:
+                        now = traced(f ^ 1, n) - own(f, k)
                     else:
-                        part = (recv[s, f ^ 1, :, block(half)] - own(f, k)) * alive[f]
-                    flux.append(part)
+                        now = own(f, k) * -alive[f]
+                    part += [now, gap]
                     if s == 2:
                         if f % 2:
                             opens = open_mask[4 * d + k : 4 * d + k + 1, :]
+                        elif f == 4:
+                            opens = pltpu.roll(open_mask[8 + k : 9 + k, :], 1, 1)
                         elif inner:
                             opens = open_mask[4 * d + n : 4 * d + n + 1, :]
                         else:
-                            opens = recv[s, f ^ 1, 54:55, block(half)]
-                        jump.append(part * opens)
-                put(late_h, late_l, 128 * d, k, jnp.concatenate(flux, axis=0))
+                            half = j if d == 0 else i
+                            opens = recv[1, f ^ 1, 54:55, block(half)]
+                        jump += [now * opens, gap]
+                put(own_h, own_l, 128 * d, k, jnp.concatenate(part, axis=0))
                 if s == 2:
                     put(jump_h, jump_l, 128 * d, k, jnp.concatenate(jump, axis=0))
-        both = mm(lb_hl[:, 0:256], late_h[...])
-        force = force + both[0:64] + both[64:128] + mm(lb_h[:, 0:256], late_l[...])
+            put(own_h, own_l, 384, k, proj[672:928, block(k)] * mod[k : k + 1, :])
+        force = mm3(lb_hl, lb_h, early, own_h, own_l)
         if s < 2:
             velocity = state[64:128, :] + substep * force
             state[64:128, :] = velocity
             state[0:64, :] = state[0:64, :] + substep * velocity
+            split_state()
+            ahead = project(slice(0, 224))
+            for f in range(4):
+                for half in range(2):
+                    k = outer[f][half]
+                    value = ahead[56 * f : 56 * f + 56, block(k)]
+                    if s == 0 and f % 2 == 1:
+                        row = 4 * (f // 2) + k
+                        value = jnp.where(row_id == 54, open_mask[row : row + 1, :], value)
+                    send[s + 1, f, :, block(half)] = value
         else:
-            both = mm(ew_hl[...], jump_h[...])
-            displace = state[0:64, :] + both[0:64] + both[64:128] + mm(ew_hl[0:64, :], jump_l[...])
+            moved = state[0:64, :] + mm3(ew_hl, ew_hl.at[0:64], slice(0, 384), jump_h, jump_l)
             for k in range(4):
-                out_u[pl.ds(k, 60, stride=4), :] = displace[0:60, block(k)]
                 out_w[pl.ds(k, 60, stride=4), :] = state[64:124, block(k)]
+
+        for d in (0, 1):
+            for side in (2 * d, 2 * d + 1):
+
+                @pl.when(there[side])
+                def _(s=s, side=side):
+                    copies[s][side ^ 1].wait_recv()
+
+            for f in (2 * d, 2 * d + 1):
+                for half in range(2):
+                    k = outer[f][half]
+                    value = came(s, f, half)
+                    if s < 2:
+                        late_h[64 * f : 64 * f + 64, block(k)] = value.astype(BF16)
+                    else:
+                        put(late_h, late_l, 64 * f, k, value)
+                        if f % 2:
+                            opens = open_mask[4 * d + k : 4 * d + k + 1, :]
+                        else:
+                            opens = recv[1, f ^ 1, 54:55, block(half)]
+                        put(leap_h, leap_l, 64 * f, k, value * opens)
+        if s < 2:
+            for i in range(2):
+                more = mm(cb[i], late_h[:, 256 * i : 256 * i + 256])
+                send[s + 1, i] = send[s + 1, i] + more[112:168]
+                for f in (2, 3):
+                    at = 56 * (f - 2)
+                    send[s + 1, f, :, block(i)] = (
+                        send[s + 1, f, :, block(i)] + more[at : at + 56, block(f - 2)]
+                    )
+            begin(s + 1, 1)
+            begin(s + 1, 0)
+        else:
+            force = force + mm3(lb_hl, lb_h, lateral, late_h, late_l)
+            moved = moved + mm3(ew_hl, ew_hl.at[0:64], lateral, leap_h, leap_l)
+            for k in range(4):
+                out_u[pl.ds(k, 60, stride=4), :] = moved[0:60, block(k)]
                 out_f[pl.ds(k, 60, stride=4), :] = force[0:60, block(k)]
 
     for s in range(3):
@@ -326,18 +386,21 @@
             pltpu.VMEM((64, 640), BF16),
             pltpu.VMEM((128, 640), BF16),
             pltpu.VMEM((128, 384), BF16),
+            pltpu.VMEM((2, 176, 256), BF16),
             pltpu.VMEM((6, 56, 128), F32),
             pltpu.VMEM((128, 256), F32),
             pltpu.VMEM((3, 128, 128), F32),
             pltpu.VMEM((3, 128, 128), F32),
             pltpu.VMEM((128, 128), F32),
             pltpu.VMEM((928, 512), F32),
+            pltpu.VMEM((640, 512), BF16),
+            pltpu.VMEM((640, 512), BF16),
+            pltpu.VMEM((256, 512), BF16),
+            pltpu.VMEM((256, 512), BF16),
             pltpu.VMEM((384, 512), BF16),
             pltpu.VMEM((384, 512), BF16),
             pltpu.VMEM((256, 512), BF16),
             pltpu.VMEM((256, 512), BF16),
-            pltpu.VMEM((384, 512), BF16),
-            pltpu.VMEM((384, 512), BF16),
             pltpu.VMEM((3, 4, 56, 256), F32),
             pltpu.VMEM((3, 4, 56, 256), F32),
             pltpu.SemaphoreType.DMA((10,)),

time: 17.7 us -> 16.8 us (0.949)
  Pallas kernels: 16.1 us -> 15.3 us
    pallas_call x1, Pallas kernels: 16.1 us -> 15.3 us  [shards(): pl.pallas_call(kernel, out_shape=(out, out, out), in_specs=[hbm] * 10, ou...]
where the time goes in v1:
time: 16.8 us; the launch traced here: 16.7 us
  Pallas kernels  15.3 us (91%)
  other arithmetic  0.72 us (4%)
  between operations  0.64 us (4%)
    pallas_call x1, Pallas kernels, shards(): pl.pallas_call(kernel, out_shape=(out, out, out), in_specs=[hbm] * 10, ou...  15.3 us
    add x1, other arithmetic, shards(): displacement_out = opened + substep * velocity_out  0.72 us

profile of v1, /device:TPU:0, one launch (start us, length us, event | category | flops | bytes accessed | tf_op | source)
XLA Modules:
  0.0 16.7 jit_solution(6824425101327451867)
XLA Ops:
  0.6 15.3 %shard_map.113 = (f32[240,128]{1,0:T(8,128)S(1)}, f32[240,128]{1,0:T(8,128)S(1)}, f32[240,128]{1,0:T(8,128)S(1)}) custom-call(f32[240,128]{1,0:T(8,128)} %bitcast.11, f32[240,128]{1,0:T(8,128)} %bitcast.12, f32[4,128]{1,0:T(4,128)} %bitcast.15, f32[60,243]{1,0:T(8,128)} %bitcast.14, f32[6,54,60]{2,1,0:T(8,128)} %trace_in.1, f32[6,54,60]{2,1,0:T(8,128)} %bitcast.8, ...), custom_call_target="tpu_custom_call" | custom-call | tf_op jit(solution)/shard_map/pallas_call | solution.py:375
  15.9 0.7 %multiply_add_fusion = (f32[240,128]{1,0:T(8,128)}, f32[240,128]{1,0:T(8,128)}) fusion(f32[240,128]{1,0:T(8,128)S(1)} %get-tuple-element.5, f32[240,128]{1,0:T(8,128)S(1)} %get-tuple-element.6, f32[240,128]{1,0:T(8,128)S(1)} %get-tuple-element.7), kind=kLoop, calls=%fused_computation | loop fusion | flops 122880 | bytes 614400 | tf_op jit(solution)/shard_map/add | solution.py:415

commit v2 on v1

--- a/solution.py
+++ b/solution.py
@@ -1,3 +1,5 @@
+import functools
+
 import jax
 import jax.numpy as jnp
 from jax import lax
@@ -47,7 +49,7 @@
     local = (trace, disp, vel, grad, lift, mod, spread, split, faces, counts)
     loads = {}
     for n, name in enumerate(names):
-        loads[name] = pltpu.make_async_copy(given[n], local[n], in_sem.at[n])
+        loads[name] = pltpu.make_async_copy(given[n], local[n], in_sem.at[0 if n < 3 else 1])
         loads[name].start()
 
     for ref in (state, tp, lp, pp, qp, gp):
@@ -79,7 +81,8 @@
         pair = [face_rows(2 * d, sign), face_rows(2 * d + 1, sign)]
         put_a(row + 112 * d, jnp.concatenate(pair, axis=0))
 
-    loads["trace"].wait()
+    for name in names[:3]:
+        loads[name].wait()
     for f in range(6):
         tp[f, 0:54, 0:60] = trace[f]
     put_faces(0, 0, 1.0)
@@ -88,8 +91,6 @@
     def block(k):
         return slice(128 * k, 128 * k + 128)
 
-    loads["disp"].wait()
-    loads["vel"].wait()
     for k in range(4):
         state[0:60, block(k)] = disp[pl.ds(k, 60, stride=4), :]
         state[64:124, block(k)] = vel[pl.ds(k, 60, stride=4), :]
@@ -99,8 +100,8 @@
             pltpu.make_async_remote_copy(
                 src_ref=send.at[s, side],
                 dst_ref=recv.at[s, side],
-                send_sem=send_sem.at[s, side],
-                recv_sem=recv_sem.at[s, side],
+                send_sem=send_sem.at[0],
+                recv_sem=recv_sem.at[s],
                 device_id=beside[side],
                 device_id_type=MESH,
             )
@@ -108,6 +109,25 @@
         ]
         for s in range(3)
     ]
+    sides = sum(t.astype(jnp.int32) for t in there)
+
+    def settle(source, target, arrival, wait):
+        for n in range(1, 5):
+            every = pltpu.make_async_remote_copy(
+                src_ref=source(n),
+                dst_ref=target(n),
+                send_sem=send_sem.at[0],
+                recv_sem=recv_sem.at[arrival],
+                device_id=beside[0],
+                device_id_type=MESH,
+            )
+            pl.when(sides == n)(functools.partial(wait, every))
+
+    def settle_arrivals(s):
+        settle(
+            lambda n: send.at[s, 0:n], lambda n: recv.at[s, 0:n], s, lambda every: every.wait_recv()
+        )
+
     outer = ((0, 1), (2, 3), (0, 2), (1, 3))
 
     def split_state():
@@ -134,7 +154,7 @@
             for half in range(2):
                 send[0, f, :, block(half)] = proj[56 * f : 56 * f + 56, block(outer[f][half])]
         if d == 1:
-            pl.semaphore_wait(barrier, sum(t.astype(jnp.int32) for t in there))
+            pl.semaphore_wait(barrier, sides)
         begin(0, d)
 
     for ref in (late_h, late_l, leap_h, leap_l):
@@ -142,7 +162,8 @@
     put_faces(0, 2, 1.0)
     for d in range(3):
         put_faces(336, d, -1.0)
-    loads["grad"].wait()
+    for name in names[3:]:
+        loads[name].wait()
     gp[0:60, 0:243] = grad[...]
     put_a(672, jnp.transpose(gp[...]))
 
@@ -154,7 +175,6 @@
         lb_hl[64:128, columns] = low
 
     put_b(384, -gp[0:64, :])
-    loads["lift"].wait()
     lift_row = lax.broadcasted_iota(jnp.int32, (54, 60), 0)
     for f in range(6):
         at = 64 * (f % 2)
@@ -172,8 +192,6 @@
         pieces = [carry[112:224], carry[56 * i : 56 * i + 56], jnp.zeros((8, 256), F32)]
         cb[i] = jnp.concatenate(pieces, axis=0).astype(BF16)
 
-    loads["spread"].wait()
-    loads["split"].wait()
     qp[0:27, 0:27] = split[...]
     qp[32:59, 0:27] = split[...]
     row128 = lax.broadcasted_iota(jnp.int32, (128, 128), 0)
@@ -192,9 +210,6 @@
         ew_hl[0:64, block(d)] = high
         ew_hl[64:128, block(d)] = low
 
-    loads["faces"].wait()
-    loads["counts"].wait()
-    loads["mod"].wait()
     ids = faces[...]
     slots = lax.broadcasted_iota(jnp.int32, ids.shape, 1)
     section = jnp.where(slots < BLK_CAP, 0, jnp.where(slots < 2 * BLK_CAP, 1, 2))
@@ -305,13 +320,8 @@
             for k in range(4):
                 out_w[pl.ds(k, 60, stride=4), :] = state[64:124, block(k)]
 
+        settle_arrivals(s)
         for d in (0, 1):
-            for side in (2 * d, 2 * d + 1):
-
-                @pl.when(there[side])
-                def _(s=s, side=side):
-                    copies[s][side ^ 1].wait_recv()
-
             for f in (2 * d, 2 * d + 1):
                 for half in range(2):
                     k = outer[f][half]
@@ -343,12 +353,9 @@
                 out_u[pl.ds(k, 60, stride=4), :] = moved[0:60, block(k)]
                 out_f[pl.ds(k, 60, stride=4), :] = force[0:60, block(k)]
 
-    for s in range(3):
-        for side in range(4):
-
-            @pl.when(there[side])
-            def _(s=s, side=side):
-                copies[s][side].wait_send()
+    settle(
+        lambda n: send.at[:, 0:n], lambda n: recv.at[:, 0:n], 0, lambda every: every.wait_send()
+    )
 
 
 def shards(
@@ -403,9 +410,9 @@
             pltpu.VMEM((256, 512), BF16),
             pltpu.VMEM((3, 4, 56, 256), F32),
             pltpu.VMEM((3, 4, 56, 256), F32),
-            pltpu.SemaphoreType.DMA((10,)),
-            pltpu.SemaphoreType.DMA((3, 4)),
-            pltpu.SemaphoreType.DMA((3, 4)),
+            pltpu.SemaphoreType.DMA((2,)),
+            pltpu.SemaphoreType.DMA((1,)),
+            pltpu.SemaphoreType.DMA((3,)),
         ],
         compiler_params=pltpu.CompilerParams(
             collective_id=0, has_side_effects=True, vmem_limit_bytes=40 * 1024 * 1024

time: 16.8 us -> 16.6 us (0.988)
  Pallas kernels: 15.3 us -> 15.1 us
    pallas_call x1, Pallas kernels: 15.3 us -> 15.1 us  [shards(): pl.pallas_call(kernel, out_shape=(out, out, out), in_specs=[hbm] * 10, ou...]
where the time goes in v2:
time: 16.6 us; the launch traced here: 16.4 us
  Pallas kernels  15.1 us (91%)
  other arithmetic  0.72 us (4%)
  between operations  0.64 us (4%)
    pallas_call x1, Pallas kernels, shards(): pl.pallas_call(kernel, out_shape=(out, out, out), in_specs=[hbm] * 10, ou...  15.1 us
    add x1, other arithmetic, shards(): displacement_out = opened + substep * velocity_out  0.72 us

profile of v2, /device:TPU:0, one launch (start us, length us, event | category | flops | bytes accessed | tf_op | source)
XLA Modules:
  0.0 16.4 jit_solution(4989658118135602086)
XLA Ops:
  0.6 15.1 %shard_map.113 = (f32[240,128]{1,0:T(8,128)S(1)}, f32[240,128]{1,0:T(8,128)S(1)}, f32[240,128]{1,0:T(8,128)S(1)}) custom-call(f32[240,128]{1,0:T(8,128)} %bitcast.11, f32[240,128]{1,0:T(8,128)} %bitcast.12, f32[4,128]{1,0:T(4,128)} %bitcast.15, f32[60,243]{1,0:T(8,128)} %bitcast.14, f32[6,54,60]{2,1,0:T(8,128)} %trace_in.1, f32[6,54,60]{2,1,0:T(8,128)} %bitcast.8, ...), custom_call_target="tpu_custom_call" | custom-call | tf_op jit(solution)/shard_map/pallas_call | solution.py:382
  15.7 0.7 %multiply_add_fusion = (f32[240,128]{1,0:T(8,128)}, f32[240,128]{1,0:T(8,128)}) fusion(f32[240,128]{1,0:T(8,128)S(1)} %get-tuple-element.5, f32[240,128]{1,0:T(8,128)S(1)} %get-tuple-element.6, f32[240,128]{1,0:T(8,128)S(1)} %get-tuple-element.7), kind=kLoop, calls=%fused_computation | loop fusion | flops 122880 | bytes 614400 | tf_op jit(solution)/shard_map/add | solution.py:422

commit v3 on v2

--- a/solution.py
+++ b/solution.py
@@ -1,5 +1,3 @@
-import functools
-
 import jax
 import jax.numpy as jnp
 from jax import lax
@@ -29,20 +27,30 @@
     disp_in, vel_in, mod_in, grad_in, trace_in, lift_in, split_in, spread_in, faces_in, counts_in,
     out_u, out_w, out_f,
     disp, vel, mod, grad, trace, lift, split, spread, faces, counts,
-    state, state_b, wa_h, wa_l, lb_h, lb_hl, ew_hl, cb, tp, gp, lp, pp, qp, proj,
+    state, state_b, wa_h, wa_l, lb_h, lb_hl, ew_hl, cy, cx, cn, known, near, tp, gp, lp, pp, qp, proj,
     own_h, own_l, late_h, late_l, jump_h, jump_l, leap_h, leap_l,
     send, recv, in_sem, send_sem, recv_sem,
 ):
     px, py = lax.axis_index("px"), lax.axis_index("py")
     nx, ny = lax.axis_size("px"), lax.axis_size("py")
-    there = (px > 0, px < nx - 1, py > 0, py < ny - 1)
-    beside = ({"px": px - 1}, {"px": px + 1}, {"py": py - 1}, {"py": py + 1})
+    odd = px % 2
+    across, partner = px - 1 + 2 * odd, px + 1 - 2 * odd
+    there = (
+        jnp.logical_and(across >= 0, across < nx), partner >= 0, py > 0, py < ny - 1,
+    )
+    beside = ({"px": across}, {"px": partner}, {"py": py - 1}, {"py": py + 1})
     barrier = pltpu.get_barrier_semaphore()
     for side in (2, 3, 0, 1):
 
         @pl.when(there[side])
         def _(side=side):
             pl.semaphore_signal(barrier, inc=1, device_id=beside[side], device_id_type=MESH)
+
+    def placed_face(f):
+        return f + odd - 2 * f * odd if f < 2 else f
+
+    def either(if_odd, if_even):
+        return jnp.where(odd == 1, if_odd, if_even)
 
     names = ("trace", "disp", "vel", "grad", "lift", "mod", "spread", "split", "faces", "counts")
     given = (trace_in, disp_in, vel_in, grad_in, lift_in, mod_in, spread_in, split_in, faces_in, counts_in)
@@ -54,12 +62,12 @@
 
     for ref in (state, tp, lp, pp, qp, gp):
         ref[...] = jnp.zeros_like(ref)
-    for slot, side in ((0, 1), (1, 0), (2, 3), (3, 2)):
-
-        @pl.when(jnp.logical_not(there[side]))
-        def _(slot=slot):
-            for s in range(3):
-                recv[s, slot] = jnp.zeros((56, 256), F32)
+    for f in range(4):
+
+        @pl.when(jnp.logical_not(there[f]))
+        def _(f=f):
+            for base in (0, 4, 8):
+                recv[base + f] = jnp.zeros((56, 256), F32)
 
     def put_a(row, value):
         high, low = halves(value)
@@ -84,7 +92,7 @@
     for name in names[:3]:
         loads[name].wait()
     for f in range(6):
-        tp[f, 0:54, 0:60] = trace[f]
+        tp[f, 0:54, 0:60] = trace[placed_face(f)]
     put_faces(0, 0, 1.0)
     put_faces(0, 1, 1.0)
 
@@ -92,41 +100,43 @@
         return slice(128 * k, 128 * k + 128)
 
     for k in range(4):
-        state[0:60, block(k)] = disp[pl.ds(k, 60, stride=4), :]
-        state[64:124, block(k)] = vel[pl.ds(k, 60, stride=4), :]
+        for row, ref in ((0, disp), (64, vel)):
+            state[row : row + 60, block(k)] = either(
+                ref[pl.ds(k ^ 2, 60, stride=4), :], ref[pl.ds(k, 60, stride=4), :]
+            )
+
+    def faced(f):
+        return f if f < 2 else f ^ 1
 
     copies = [
-        [
-            pltpu.make_async_remote_copy(
-                src_ref=send.at[s, side],
-                dst_ref=recv.at[s, side],
+        pltpu.make_async_remote_copy(
+            src_ref=send.at[slot],
+            dst_ref=recv.at[slot - slot % 4 + faced(slot % 4)],
+            send_sem=send_sem.at[0],
+            recv_sem=recv_sem.at[slot // 2],
+            device_id=beside[slot % 4],
+            device_id_type=MESH,
+        )
+        for slot in range(12)
+    ]
+
+    def begin(*slots):
+        for slot in slots:
+            pl.when(there[slot % 4])(copies[slot].start)
+
+    def settle(pair):
+        first = there[pair % 2 * 2].astype(jnp.int32)
+        both = first + there[pair % 2 * 2 + 1].astype(jnp.int32)
+        for n in (1, 2):
+            every = pltpu.make_async_remote_copy(
+                src_ref=send.at[0:n],
+                dst_ref=recv.at[0:n],
                 send_sem=send_sem.at[0],
-                recv_sem=recv_sem.at[s],
-                device_id=beside[side],
+                recv_sem=recv_sem.at[pair],
+                device_id=beside[1],
                 device_id_type=MESH,
             )
-            for side in range(4)
-        ]
-        for s in range(3)
-    ]
-    sides = sum(t.astype(jnp.int32) for t in there)
-
-    def settle(source, target, arrival, wait):
-        for n in range(1, 5):
-            every = pltpu.make_async_remote_copy(
-                src_ref=source(n),
-                dst_ref=target(n),
-                send_sem=send_sem.at[0],
-                recv_sem=recv_sem.at[arrival],
-                device_id=beside[0],
-                device_id_type=MESH,
-            )
-            pl.when(sides == n)(functools.partial(wait, every))
-
-    def settle_arrivals(s):
-        settle(
-            lambda n: send.at[s, 0:n], lambda n: recv.at[s, 0:n], s, lambda every: every.wait_recv()
-        )
+            pl.when(both == n)(every.wait_recv)
 
     outer = ((0, 1), (2, 3), (0, 2), (1, 3))
 
@@ -138,13 +148,6 @@
 
     def project(rows):
         return mm(wa_h[rows, :], state_b[...]) + mm(wa_l[rows, :], state_b[0:128, :])
-
-    def begin(s, d):
-        for side in (2 * d, 2 * d + 1):
-
-            @pl.when(there[side])
-            def _(side=side):
-                copies[s][side].start()
 
     split_state()
     for d in (1, 0):
@@ -152,11 +155,10 @@
         proj[rows, :] = project(rows)
         for f in (2 * d, 2 * d + 1):
             for half in range(2):
-                send[0, f, :, block(half)] = proj[56 * f : 56 * f + 56, block(outer[f][half])]
+                send[f, :, block(half)] = proj[56 * f : 56 * f + 56, block(outer[f][half])]
         if d == 1:
-            pl.semaphore_wait(barrier, sides)
-        begin(0, d)
-
+            pl.semaphore_wait(barrier, sum(t.astype(jnp.int32) for t in there))
+        begin(2 * d, 2 * d + 1)
     for ref in (late_h, late_l, leap_h, leap_l):
         ref[...] = jnp.zeros_like(ref)
     put_faces(0, 2, 1.0)
@@ -178,7 +180,9 @@
     lift_row = lax.broadcasted_iota(jnp.int32, (54, 60), 0)
     for f in range(6):
         at = 64 * (f % 2)
-        lp[f // 2, at : at + 54, 0:60] = jnp.where(lift_row < 27, lift[f], 0.5 * lift[f])
+        lp[f // 2, at : at + 54, 0:60] = jnp.where(
+            lift_row < 27, lift[placed_face(f)], 0.5 * lift[placed_face(f)]
+        )
     for d in range(3):
         put_b(128 * d, jnp.transpose(lp[d])[0:64, :])
 
@@ -188,9 +192,12 @@
         reach.append((substep * substep) * rows + substep * pltpu.roll(rows, 64, 1))
     high, low = halves(jnp.concatenate(reach, axis=0)[:, 0:64])
     carry = mm(high, lb_h[:, 0:256]) + mm(low, lb_h[:, 0:256]) + mm(high, lb_hl[64:128, 0:256])
-    for i in range(2):
-        pieces = [carry[112:224], carry[56 * i : 56 * i + 56], jnp.zeros((8, 256), F32)]
-        cb[i] = jnp.concatenate(pieces, axis=0).astype(BF16)
+    cy[...] = carry[112:224, 0:128].astype(BF16)
+    cx[...] = carry[0:112, 128:256].astype(BF16)
+    for f in range(4):
+        o = f ^ 1
+        pieces = [carry[56 * o : 56 * o + 56, 64 * o : 64 * o + 64], jnp.zeros((8, 64), F32)]
+        cn[f] = jnp.concatenate(pieces, axis=0).astype(BF16)
 
     qp[0:27, 0:27] = split[...]
     qp[32:59, 0:27] = split[...]
@@ -198,7 +205,7 @@
     placed = jnp.where(row128 < 32, pltpu.roll(qp[...], 27, 1), pltpu.roll(qp[...], 91, 1))
     for f in range(6):
         at = 32 * (f % 2)
-        pp[f // 2, at : at + 27, 0:60] = spread[f]
+        pp[f // 2, at : at + 27, 0:60] = spread[placed_face(f)]
     for d in range(3):
         part = jnp.dot(
             jnp.transpose(pp[d])[0:64, :],
@@ -218,7 +225,9 @@
         counts[0:1, 0:1],
         jnp.where(section == 1, BLK_CAP + counts[0:1, 1:2], 2 * BLK_CAP + counts[0:1, 2:3]),
     )
-    group = jnp.where(slots < limit, ids >> 7, -1)
+    group = ids >> 7
+    group = jnp.where(group < 4, group, (group & 12) + ((group + 2 * odd) & 3))
+    group = jnp.where(slots < limit, group, -1)
     spot = ids & 127
     high_hot = lax.broadcasted_iota(jnp.int32, (16, ids.shape[1]), 0) == group
     low_hot = lax.broadcasted_iota(jnp.int32, (128, ids.shape[1]), 0) == spot
@@ -249,13 +258,38 @@
         return proj[336 + 56 * f : 392 + 56 * f, block(k)]
 
     def came(s, f, half):
-        return jnp.concatenate([recv[s, f ^ 1, :, block(half)], gap], axis=0)
+        value = recv[4 * s + f, :, block(half)]
+        if s > 0:
+            value = value + known[f, 0:56, block(half)]
+        return jnp.concatenate([value, gap], axis=0)
+
+    def arrive(s, f):
+        for half in range(2):
+            value = came(s, f, half)
+            late_h[64 * f : 64 * f + 64, block(outer[f][half])] = value.astype(BF16)
+
+    def opens(f, k):
+        i, j = k // 2, k % 2
+        n = k if f > 3 else k ^ (2 - f // 2)
+        inner = f > 3 or (i, 1 - i, j, 1 - j)[f] == 1
+        if f == 4:
+            return pltpu.roll(open_mask[8 + k : 9 + k, :], 1, 1)
+        if f in (3, 5):
+            row = 4 * (f // 2) + k
+            return open_mask[row : row + 1, :]
+        if f == 2:
+            return open_mask[4 + n : 5 + n, :] if inner else recv[6, 54:55, block(i)]
+        if inner:
+            return open_mask[j : j + 1, :]
+        mine, other = open_mask[2 + j : 3 + j, :], recv[4 + f, 54:55, block(j)]
+        return either(mine, other) if f == 0 else either(other, mine)
 
     def mm3(both_ref, high_ref, columns, b_high, b_low):
         both = mm(both_ref[:, columns], b_high[...])
         return both[0:64] + both[64:128] + mm(high_ref[:, columns], b_low[...])
 
     early, lateral = slice(0, 640), slice(0, 256)
+    moduli = [either(mod[k ^ 2 : (k ^ 2) + 1, :], mod[k : k + 1, :]) for k in range(4)]
     for s in range(3):
         if s > 0:
             for f in range(4):
@@ -267,6 +301,11 @@
             state[64:128, :] = state[64:128, :] + substep * force
             state[0:64, :] = state[0:64, :] + (substep * substep) * force
             split_state()
+            for f in range(4):
+                for half in range(2):
+                    value = traced(f, outer[f][half]) * alive[f]
+                    near[f, :, block(half)] = jnp.concatenate([value, gap], axis=0).astype(BF16)
+                known[f] = mm(cn[f], near[f])
         todo = slice(224 if s == 0 else 0, 928)
         proj[todo, :] = project(todo)
         for k in range(4):
@@ -286,20 +325,11 @@
                         now = own(f, k) * -alive[f]
                     part += [now, gap]
                     if s == 2:
-                        if f % 2:
-                            opens = open_mask[4 * d + k : 4 * d + k + 1, :]
-                        elif f == 4:
-                            opens = pltpu.roll(open_mask[8 + k : 9 + k, :], 1, 1)
-                        elif inner:
-                            opens = open_mask[4 * d + n : 4 * d + n + 1, :]
-                        else:
-                            half = j if d == 0 else i
-                            opens = recv[1, f ^ 1, 54:55, block(half)]
-                        jump += [now * opens, gap]
+                        jump += [now * opens(f, k), gap]
                 put(own_h, own_l, 128 * d, k, jnp.concatenate(part, axis=0))
                 if s == 2:
                     put(jump_h, jump_l, 128 * d, k, jnp.concatenate(jump, axis=0))
-            put(own_h, own_l, 384, k, proj[672:928, block(k)] * mod[k : k + 1, :])
+            put(own_h, own_l, 384, k, proj[672:928, block(k)] * moduli[k])
         force = mm3(lb_hl, lb_h, early, own_h, own_l)
         if s < 2:
             velocity = state[64:128, :] + substep * force
@@ -311,51 +341,67 @@
                 for half in range(2):
                     k = outer[f][half]
                     value = ahead[56 * f : 56 * f + 56, block(k)]
-                    if s == 0 and f % 2 == 1:
-                        row = 4 * (f // 2) + k
+                    if s == 0 and f != 2:
+                        row = 4 + k if f == 3 else 2 + half
                         value = jnp.where(row_id == 54, open_mask[row : row + 1, :], value)
-                    send[s + 1, f, :, block(half)] = value
+                    send[4 * s + 4 + f, :, block(half)] = value
         else:
             moved = state[0:64, :] + mm3(ew_hl, ew_hl.at[0:64], slice(0, 384), jump_h, jump_l)
             for k in range(4):
-                out_w[pl.ds(k, 60, stride=4), :] = state[64:124, block(k)]
-
-        settle_arrivals(s)
-        for d in (0, 1):
-            for f in (2 * d, 2 * d + 1):
+                out_w[pl.ds(k, 60, stride=4), :] = either(
+                    state[64:124, block(k ^ 2)], state[64:124, block(k)]
+                )
+
+        if s < 2:
+            then = 4 * s + 4
+            settle(2 * s)
+            for f in (1, 0):
+                arrive(s, f)
+            more = mm(cy[...], late_h[0:128, :])
+            for f in (2, 3):
+                at = 56 * (f - 2)
+                for half in range(2):
+                    send[then + f, :, block(half)] = (
+                        send[then + f, :, block(half)] + more[at : at + 56, block(outer[f][half])]
+                    )
+            begin(then + 2, then + 3)
+            settle(2 * s + 1)
+            for f in (2, 3):
+                arrive(s, f)
+            more = mm(cx[...], late_h[128:256, :])
+            for f in (0, 1):
+                at = 56 * f
+                send[then + f] = send[then + f] + more[at : at + 56, 256 * f : 256 * f + 256]
+            begin(then, then + 1)
+        else:
+            settle(4)
+            settle(5)
+            for f in range(4):
                 for half in range(2):
                     k = outer[f][half]
-                    value = came(s, f, half)
-                    if s < 2:
-                        late_h[64 * f : 64 * f + 64, block(k)] = value.astype(BF16)
-                    else:
-                        put(late_h, late_l, 64 * f, k, value)
-                        if f % 2:
-                            opens = open_mask[4 * d + k : 4 * d + k + 1, :]
-                        else:
-                            opens = recv[1, f ^ 1, 54:55, block(half)]
-                        put(leap_h, leap_l, 64 * f, k, value * opens)
-        if s < 2:
-            for i in range(2):
-                more = mm(cb[i], late_h[:, 256 * i : 256 * i + 256])
-                send[s + 1, i] = send[s + 1, i] + more[112:168]
-                for f in (2, 3):
-                    at = 56 * (f - 2)
-                    send[s + 1, f, :, block(i)] = (
-                        send[s + 1, f, :, block(i)] + more[at : at + 56, block(f - 2)]
-                    )
-            begin(s + 1, 1)
-            begin(s + 1, 0)
-        else:
+                    value = came(2, f, half)
+                    put(late_h, late_l, 64 * f, k, value)
+                    put(leap_h, leap_l, 64 * f, k, value * opens(f, k))
             force = force + mm3(lb_hl, lb_h, lateral, late_h, late_l)
             moved = moved + mm3(ew_hl, ew_hl.at[0:64], lateral, leap_h, leap_l)
             for k in range(4):
-                out_u[pl.ds(k, 60, stride=4), :] = moved[0:60, block(k)]
-                out_f[pl.ds(k, 60, stride=4), :] = force[0:60, block(k)]
-
-    settle(
-        lambda n: send.at[:, 0:n], lambda n: recv.at[:, 0:n], 0, lambda every: every.wait_send()
-    )
+                out_u[pl.ds(k, 60, stride=4), :] = either(
+                    moved[0:60, block(k ^ 2)], moved[0:60, block(k)]
+                )
+                out_f[pl.ds(k, 60, stride=4), :] = either(
+                    force[0:60, block(k ^ 2)], force[0:60, block(k)]
+                )
+
+    for n in range(1, 5):
+        every = pltpu.make_async_remote_copy(
+            src_ref=send.at[0 : 3 * n],
+            dst_ref=recv.at[0 : 3 * n],
+            send_sem=send_sem.at[0],
+            recv_sem=recv_sem.at[0],
+            device_id=beside[1],
+            device_id_type=MESH,
+        )
+        pl.when(sum(t.astype(jnp.int32) for t in there) == n)(every.wait_send)
 
 
 def shards(
@@ -393,7 +439,11 @@
             pltpu.VMEM((64, 640), BF16),
             pltpu.VMEM((128, 640), BF16),
             pltpu.VMEM((128, 384), BF16),
-            pltpu.VMEM((2, 176, 256), BF16),
+            pltpu.VMEM((112, 128), BF16),
+            pltpu.VMEM((112, 128), BF16),
+            pltpu.VMEM((4, 64, 64), BF16),
+            pltpu.VMEM((4, 64, 256), F32),
+            pltpu.VMEM((4, 64, 256), BF16),
             pltpu.VMEM((6, 56, 128), F32),
             pltpu.VMEM((128, 256), F32),
             pltpu.VMEM((3, 128, 128), F32),
@@ -408,11 +458,11 @@
             pltpu.VMEM((384, 512), BF16),
             pltpu.VMEM((256, 512), BF16),
             pltpu.VMEM((256, 512), BF16),
-            pltpu.VMEM((3, 4, 56, 256), F32),
-            pltpu.VMEM((3, 4, 56, 256), F32),
+            pltpu.VMEM((12, 56, 256), F32),
+            pltpu.VMEM((12, 56, 256), F32),
             pltpu.SemaphoreType.DMA((2,)),
             pltpu.SemaphoreType.DMA((1,)),
-            pltpu.SemaphoreType.DMA((3,)),
+            pltpu.SemaphoreType.DMA((6,)),
         ],
         compiler_params=pltpu.CompilerParams(
             collective_id=0, has_side_effects=True, vmem_limit_bytes=40 * 1024 * 1024

time: 16.6 us -> 15.3 us (0.922)
  the two profiles are of different devices: /device:TPU:0 before, /device:TPU:5 now
where the time goes in v3:
time: 15.3 us; the launch traced here: 15.1 us
  Pallas kernels  13.7 us (90%)
  other arithmetic  0.72 us (5%)
  between operations  0.64 us (4%)
    pallas_call x1, Pallas kernels, shards(): pl.pallas_call(kernel, out_shape=(out, out, out), in_specs=[hbm] * 10, ou...  13.7 us
    add x1, other arithmetic, shards(): displacement_out = opened + substep * velocity_out  0.72 us

profile of v3, /device:TPU:5, one launch (start us, length us, event | category | flops | bytes accessed | tf_op | source)
XLA Modules:
  0.0 15.1 jit_solution(11617298267535344468)
XLA Ops:
  0.6 13.7 %shard_map.113 = (f32[240,128]{1,0:T(8,128)S(1)}, f32[240,128]{1,0:T(8,128)S(1)}, f32[240,128]{1,0:T(8,128)S(1)}) custom-call(f32[240,128]{1,0:T(8,128)} %bitcast.11, f32[240,128]{1,0:T(8,128)} %bitcast.12, f32[4,128]{1,0:T(4,128)} %bitcast.15, f32[60,243]{1,0:T(8,128)} %bitcast.14, f32[6,54,60]{2,1,0:T(8,128)} %trace_in.1, f32[6,54,60]{2,1,0:T(8,128)} %bitcast.8, ...), custom_call_target="tpu_custom_call" | custom-call | tf_op jit(solution)/shard_map/pallas_call | solution.py:428
  14.4 0.7 %multiply_add_fusion = (f32[240,128]{1,0:T(8,128)}, f32[240,128]{1,0:T(8,128)}) fusion(f32[240,128]{1,0:T(8,128)S(1)} %get-tuple-element.5, f32[240,128]{1,0:T(8,128)S(1)} %get-tuple-element.6, f32[240,128]{1,0:T(8,128)S(1)} %get-tuple-element.7), kind=kLoop, calls=%fused_computation | loop fusion | flops 122880 | bytes 614400 | tf_op jit(solution)/shard_map/add | solution.py:472

commit v4 on v3

--- a/solution.py
+++ b/solution.py
@@ -108,31 +108,31 @@
     def faced(f):
         return f if f < 2 else f ^ 1
 
-    copies = [
-        pltpu.make_async_remote_copy(
-            src_ref=send.at[slot],
-            dst_ref=recv.at[slot - slot % 4 + faced(slot % 4)],
+    def copy(slot, columns=slice(0, 256)):
+        return pltpu.make_async_remote_copy(
+            src_ref=send.at[slot, :, columns],
+            dst_ref=recv.at[slot - slot % 4 + faced(slot % 4), :, columns],
             send_sem=send_sem.at[0],
-            recv_sem=recv_sem.at[slot // 2],
+            recv_sem=recv_sem.at[slot // 4, (0, 1, 2, 2)[slot % 4]],
             device_id=beside[slot % 4],
             device_id_type=MESH,
         )
-        for slot in range(12)
-    ]
-
-    def begin(*slots):
+
+    def begin(*slots, columns=slice(0, 256)):
         for slot in slots:
-            pl.when(there[slot % 4])(copies[slot].start)
-
-    def settle(pair):
-        first = there[pair % 2 * 2].astype(jnp.int32)
-        both = first + there[pair % 2 * 2 + 1].astype(jnp.int32)
+            pl.when(there[slot % 4])(copy(slot, columns).start)
+
+    def settle_x(s, f):
+        pl.when(there[f])(copy(4 * s + f).wait_recv)
+
+    def settle_y(s):
+        both = there[2].astype(jnp.int32) + there[3].astype(jnp.int32)
         for n in (1, 2):
             every = pltpu.make_async_remote_copy(
                 src_ref=send.at[0:n],
                 dst_ref=recv.at[0:n],
                 send_sem=send_sem.at[0],
-                recv_sem=recv_sem.at[pair],
+                recv_sem=recv_sem.at[s, 2],
                 device_id=beside[1],
                 device_id_type=MESH,
             )
@@ -354,28 +354,43 @@
 
         if s < 2:
             then = 4 * s + 4
-            settle(2 * s)
-            for f in (1, 0):
+            def after_x(f, s=s, then=then):
+                settle_x(s, f)
                 arrive(s, f)
-            more = mm(cy[...], late_h[0:128, :])
-            for f in (2, 3):
-                at = 56 * (f - 2)
-                for half in range(2):
-                    send[then + f, :, block(half)] = (
-                        send[then + f, :, block(half)] + more[at : at + 56, block(outer[f][half])]
+                more = mm(cy[...], late_h[0:128, 256 * f : 256 * f + 256])
+                for y in (2, 3):
+                    at = 56 * (y - 2)
+                    send[then + y, :, block(f)] = (
+                        send[then + y, :, block(f)] + more[at : at + 56, block(y - 2)]
                     )
-            begin(then + 2, then + 3)
-            settle(2 * s + 1)
-            for f in (2, 3):
-                arrive(s, f)
-            more = mm(cx[...], late_h[128:256, :])
-            for f in (0, 1):
-                at = 56 * f
-                send[then + f] = send[then + f] + more[at : at + 56, 256 * f : 256 * f + 256]
-            begin(then, then + 1)
+                begin(then + 2, then + 3, columns=block(f))
+
+            def after_y(s=s, then=then):
+                settle_y(s)
+                for f in (2, 3):
+                    arrive(s, f)
+                more = mm(cx[...], late_h[128:256, :])
+                for f in (0, 1):
+                    at = 56 * f
+                    send[then + f] = send[then + f] + more[at : at + 56, 256 * f : 256 * f + 256]
+                begin(then, then + 1)
+
+            after_x(1)
+
+            @pl.when(odd == 0)
+            def _():
+                after_x(0)
+                after_y()
+
+            @pl.when(odd == 1)
+            def _():
+                after_y()
+                after_x(0)
+
         else:
-            settle(4)
-            settle(5)
+            settle_x(2, 1)
+            settle_y(2)
+            settle_x(2, 0)
             for f in range(4):
                 for half in range(2):
                     k = outer[f][half]
@@ -397,7 +412,7 @@
             src_ref=send.at[0 : 3 * n],
             dst_ref=recv.at[0 : 3 * n],
             send_sem=send_sem.at[0],
-            recv_sem=recv_sem.at[0],
+            recv_sem=recv_sem.at[0, 0],
             device_id=beside[1],
             device_id_type=MESH,
         )
@@ -462,7 +477,7 @@
             pltpu.VMEM((12, 56, 256), F32),
             pltpu.SemaphoreType.DMA((2,)),
             pltpu.SemaphoreType.DMA((1,)),
-            pltpu.SemaphoreType.DMA((6,)),
+            pltpu.SemaphoreType.DMA((3, 3)),
         ],
         compiler_params=pltpu.CompilerParams(
             collective_id=0, has_side_effects=True, vmem_limit_bytes=40 * 1024 * 1024

time: 15.3 us -> 14.7 us (0.961)
  the two profiles are of different devices: /device:TPU:5 before, /device:TPU:1 now
where the time goes in v4:
time: 14.7 us; the launch traced here: 14.5 us
  Pallas kernels  13.2 us (90%)
  other arithmetic  0.72 us (5%)
  between operations  0.64 us (4%)
    pallas_call x1, Pallas kernels, shards(): pl.pallas_call(kernel, out_shape=(out, out, out), in_specs=[hbm] * 10, ou...  13.2 us
    add x1, other arithmetic, shards(): displacement_out = opened + substep * velocity_out  0.72 us

profile of v4, /device:TPU:1, one launch (start us, length us, event | category | flops | bytes accessed | tf_op | source)
XLA Modules:
  0.0 14.5 jit_solution(12857660075999130373)
XLA Ops:
  0.6 13.2 %shard_map.113 = (f32[240,128]{1,0:T(8,128)S(1)}, f32[240,128]{1,0:T(8,128)S(1)}, f32[240,128]{1,0:T(8,128)S(1)}) custom-call(f32[240,128]{1,0:T(8,128)} %bitcast.11, f32[240,128]{1,0:T(8,128)} %bitcast.12, f32[4,128]{1,0:T(4,128)} %bitcast.15, f32[60,243]{1,0:T(8,128)} %bitcast.14, f32[6,54,60]{2,1,0:T(8,128)} %trace_in.1, f32[6,54,60]{2,1,0:T(8,128)} %bitcast.8, ...), custom_call_target="tpu_custom_call" | custom-call | tf_op jit(solution)/shard_map/pallas_call | solution.py:443
  13.8 0.7 %multiply_add_fusion = (f32[240,128]{1,0:T(8,128)}, f32[240,128]{1,0:T(8,128)}) fusion(f32[240,128]{1,0:T(8,128)S(1)} %get-tuple-element.5, f32[240,128]{1,0:T(8,128)S(1)} %get-tuple-element.6, f32[240,128]{1,0:T(8,128)S(1)} %get-tuple-element.7), kind=kLoop, calls=%fused_computation | loop fusion | flops 122880 | bytes 614400 | tf_op jit(solution)/shard_map/add | solution.py:487

commit v5 on v4

--- a/solution.py
+++ b/solution.py
@@ -28,7 +28,7 @@
     out_u, out_w, out_f,
     disp, vel, mod, grad, trace, lift, split, spread, faces, counts,
     state, state_b, wa_h, wa_l, lb_h, lb_hl, ew_hl, cy, cx, cn, known, near, tp, gp, lp, pp, qp, proj,
-    own_h, own_l, late_h, late_l, jump_h, jump_l, leap_h, leap_l,
+    own_h, own_l, late_h, late_l, jump_h, jump_l, leap, e2,
     send, recv, in_sem, send_sem, recv_sem,
 ):
     px, py = lax.axis_index("px"), lax.axis_index("py")
@@ -57,8 +57,9 @@
     local = (trace, disp, vel, grad, lift, mod, spread, split, faces, counts)
     loads = {}
     for n, name in enumerate(names):
-        loads[name] = pltpu.make_async_copy(given[n], local[n], in_sem.at[0 if n < 3 else 1])
-        loads[name].start()
+        loads[name] = pltpu.make_async_copy(given[n], local[n], in_sem.at[0])
+        if n < 3:
+            loads[name].start()
 
     for ref in (state, tp, lp, pp, qp, gp):
         ref[...] = jnp.zeros_like(ref)
@@ -91,6 +92,8 @@
 
     for name in names[:3]:
         loads[name].wait()
+    for name in names[3:]:
+        loads[name].start()
     for f in range(6):
         tp[f, 0:54, 0:60] = trace[placed_face(f)]
     put_faces(0, 0, 1.0)
@@ -113,7 +116,7 @@
             src_ref=send.at[slot, :, columns],
             dst_ref=recv.at[slot - slot % 4 + faced(slot % 4), :, columns],
             send_sem=send_sem.at[0],
-            recv_sem=recv_sem.at[slot // 4, (0, 1, 2, 2)[slot % 4]],
+            recv_sem=recv_sem.at[min(slot // 4 * 3 + (0, 1, 2, 2)[slot % 4], 6)],
             device_id=beside[slot % 4],
             device_id_type=MESH,
         )
@@ -132,7 +135,7 @@
                 src_ref=send.at[0:n],
                 dst_ref=recv.at[0:n],
                 send_sem=send_sem.at[0],
-                recv_sem=recv_sem.at[s, 2],
+                recv_sem=recv_sem.at[3 * s + 2],
                 device_id=beside[1],
                 device_id_type=MESH,
             )
@@ -150,16 +153,14 @@
         return mm(wa_h[rows, :], state_b[...]) + mm(wa_l[rows, :], state_b[0:128, :])
 
     split_state()
-    for d in (1, 0):
-        rows = slice(112 * d, 112 * d + 112)
-        proj[rows, :] = project(rows)
-        for f in (2 * d, 2 * d + 1):
-            for half in range(2):
-                send[f, :, block(half)] = proj[56 * f : 56 * f + 56, block(outer[f][half])]
-        if d == 1:
-            pl.semaphore_wait(barrier, sum(t.astype(jnp.int32) for t in there))
-        begin(2 * d, 2 * d + 1)
-    for ref in (late_h, late_l, leap_h, leap_l):
+    proj[0:224, :] = project(slice(0, 224))
+    for f in range(4):
+        for half in range(2):
+            send[f, :, block(half)] = proj[56 * f : 56 * f + 56, block(outer[f][half])]
+    pl.semaphore_wait(barrier, sum(t.astype(jnp.int32) for t in there))
+    begin(0, 2, 3, 1)
+
+    for ref in (late_h, late_l, leap):
         ref[...] = jnp.zeros_like(ref)
     put_faces(0, 2, 1.0)
     for d in range(3):
@@ -206,6 +207,8 @@
     for f in range(6):
         at = 32 * (f % 2)
         pp[f // 2, at : at + 27, 0:60] = spread[placed_face(f)]
+    lane64 = lax.broadcasted_iota(jnp.int32, (64, 128), 1)
+    packed = jnp.zeros((64, 128), F32)
     for d in range(3):
         part = jnp.dot(
             jnp.transpose(pp[d])[0:64, :],
@@ -216,6 +219,15 @@
         high, low = halves(-part)
         ew_hl[0:64, block(d)] = high
         ew_hl[64:128, block(d)] = low
+        if d < 2:
+            first = jnp.where(lane64 < 64, -part, 0.0)
+            packed += pltpu.roll(first, (104, 40)[d], 1)
+            packed += pltpu.roll(-part - first, (72, 8)[d], 1)
+    high, low = halves(packed)
+    e2[0:64, 0:128] = high
+    e2[0:64, 128:256] = high
+    e2[64:128, 0:128] = low
+    e2[64:128, 128:256] = jnp.zeros((64, 128), BF16)
 
     ids = faces[...]
     slots = lax.broadcasted_iota(jnp.int32, ids.shape, 1)
@@ -388,17 +400,28 @@
                 after_x(0)
 
         else:
-            settle_x(2, 1)
-            settle_y(2)
-            settle_x(2, 0)
+            every_side = sum(t.astype(jnp.int32) for t in there)
+            for n in range(1, 5):
+                every = pltpu.make_async_remote_copy(
+                    src_ref=send.at[0:n],
+                    dst_ref=recv.at[0:n],
+                    send_sem=send_sem.at[0],
+                    recv_sem=recv_sem.at[6],
+                    device_id=beside[1],
+                    device_id_type=MESH,
+                )
+                pl.when(every_side == n)(every.wait_recv)
             for f in range(4):
                 for half in range(2):
                     k = outer[f][half]
                     value = came(2, f, half)
                     put(late_h, late_l, 64 * f, k, value)
-                    put(leap_h, leap_l, 64 * f, k, value * opens(f, k))
+                    high, low = halves(value[24:56] * opens(f, k))
+                    leap[32 * f : 32 * f + 32, block(k)] = high
+                    leap[128 + 32 * f : 160 + 32 * f, block(k)] = low
             force = force + mm3(lb_hl, lb_h, lateral, late_h, late_l)
-            moved = moved + mm3(ew_hl, ew_hl.at[0:64], lateral, leap_h, leap_l)
+            both = mm(e2[...], leap[...])
+            moved = moved + both[0:64] + both[64:128]
             for k in range(4):
                 out_u[pl.ds(k, 60, stride=4), :] = either(
                     moved[0:60, block(k ^ 2)], moved[0:60, block(k)]
@@ -412,7 +435,7 @@
             src_ref=send.at[0 : 3 * n],
             dst_ref=recv.at[0 : 3 * n],
             send_sem=send_sem.at[0],
-            recv_sem=recv_sem.at[0, 0],
+            recv_sem=recv_sem.at[0],
             device_id=beside[1],
             device_id_type=MESH,
         )
@@ -472,12 +495,12 @@
             pltpu.VMEM((384, 512), BF16),
             pltpu.VMEM((384, 512), BF16),
             pltpu.VMEM((256, 512), BF16),
-            pltpu.VMEM((256, 512), BF16),
+            pltpu.VMEM((128, 256), BF16),
             pltpu.VMEM((12, 56, 256), F32),
             pltpu.VMEM((12, 56, 256), F32),
-            pltpu.SemaphoreType.DMA((2,)),
             pltpu.SemaphoreType.DMA((1,)),
-            pltpu.SemaphoreType.DMA((3, 3)),
+            pltpu.SemaphoreType.DMA((1,)),
+            pltpu.SemaphoreType.DMA((7,)),
         ],
         compiler_params=pltpu.CompilerParams(
             collective_id=0, has_side_effects=True, vmem_limit_bytes=40 * 1024 * 1024

time: 14.7 us -> 14.7 us (level)
  no operation moved by 1% of the time
where the time goes in v5:
time: 14.7 us; the launch traced here: 14.6 us
  Pallas kernels  13.2 us (90%)
  other arithmetic  0.72 us (5%)
  between operations  0.64 us (4%)
    pallas_call x1, Pallas kernels, shards(): pl.pallas_call(kernel, out_shape=(out, out, out), in_specs=[hbm] * 10, ou...  13.2 us
    add x1, other arithmetic, shards(): displacement_out = opened + substep * velocity_out  0.72 us

profile of v5, /device:TPU:1, one launch (start us, length us, event | category | flops | bytes accessed | tf_op | source)
XLA Modules:
  0.0 14.6 jit_solution(14509297492137680657)
XLA Ops:
  0.6 13.2 %shard_map.113 = (f32[240,128]{1,0:T(8,128)S(1)}, f32[240,128]{1,0:T(8,128)S(1)}, f32[240,128]{1,0:T(8,128)S(1)}) custom-call(f32[240,128]{1,0:T(8,128)} %bitcast.11, f32[240,128]{1,0:T(8,128)} %bitcast.12, f32[4,128]{1,0:T(4,128)} %bitcast.15, f32[60,243]{1,0:T(8,128)} %bitcast.14, f32[6,54,60]{2,1,0:T(8,128)} %trace_in.1, f32[6,54,60]{2,1,0:T(8,128)} %bitcast.8, ...), custom_call_target="tpu_custom_call" | custom-call | tf_op jit(solution)/shard_map/pallas_call | solution.py:466
  13.8 0.7 %multiply_add_fusion = (f32[240,128]{1,0:T(8,128)}, f32[240,128]{1,0:T(8,128)}) fusion(f32[240,128]{1,0:T(8,128)S(1)} %get-tuple-element.5, f32[240,128]{1,0:T(8,128)S(1)} %get-tuple-element.6, f32[240,128]{1,0:T(8,128)S(1)} %get-tuple-element.7), kind=kLoop, calls=%fused_computation | loop fusion | flops 122880 | bytes 614400 | tf_op jit(solution)/shard_map/add | solution.py:510

commit v6 on v5

--- a/solution.py
+++ b/solution.py
@@ -57,9 +57,8 @@
     local = (trace, disp, vel, grad, lift, mod, spread, split, faces, counts)
     loads = {}
     for n, name in enumerate(names):
-        loads[name] = pltpu.make_async_copy(given[n], local[n], in_sem.at[0])
-        if n < 3:
-            loads[name].start()
+        loads[name] = pltpu.make_async_copy(given[n], local[n], in_sem.at[0 if n < 3 else 1])
+        loads[name].start()
 
     for ref in (state, tp, lp, pp, qp, gp):
         ref[...] = jnp.zeros_like(ref)
@@ -92,8 +91,6 @@
 
     for name in names[:3]:
         loads[name].wait()
-    for name in names[3:]:
-        loads[name].start()
     for f in range(6):
         tp[f, 0:54, 0:60] = trace[placed_face(f)]
     put_faces(0, 0, 1.0)
@@ -153,13 +150,15 @@
         return mm(wa_h[rows, :], state_b[...]) + mm(wa_l[rows, :], state_b[0:128, :])
 
     split_state()
-    proj[0:224, :] = project(slice(0, 224))
-    for f in range(4):
-        for half in range(2):
-            send[f, :, block(half)] = proj[56 * f : 56 * f + 56, block(outer[f][half])]
-    pl.semaphore_wait(barrier, sum(t.astype(jnp.int32) for t in there))
-    begin(0, 2, 3, 1)
-
+    for d in (1, 0):
+        rows = slice(112 * d, 112 * d + 112)
+        proj[rows, :] = project(rows)
+        for f in (2 * d, 2 * d + 1):
+            for half in range(2):
+                send[f, :, block(half)] = proj[56 * f : 56 * f + 56, block(outer[f][half])]
+        if d == 1:
+            pl.semaphore_wait(barrier, sum(t.astype(jnp.int32) for t in there))
+        begin(2 * d, 2 * d + 1)
     for ref in (late_h, late_l, leap):
         ref[...] = jnp.zeros_like(ref)
     put_faces(0, 2, 1.0)
@@ -194,7 +193,9 @@
     high, low = halves(jnp.concatenate(reach, axis=0)[:, 0:64])
     carry = mm(high, lb_h[:, 0:256]) + mm(low, lb_h[:, 0:256]) + mm(high, lb_hl[64:128, 0:256])
     cy[...] = carry[112:224, 0:128].astype(BF16)
-    cx[...] = carry[0:112, 128:256].astype(BF16)
+    for f in range(2):
+        pieces = [carry[56 * f : 56 * f + 56, 128:256], jnp.zeros((8, 128), F32)]
+        cx[f] = jnp.concatenate(pieces, axis=0).astype(BF16)
     for f in range(4):
         o = f ^ 1
         pieces = [carry[56 * o : 56 * o + 56, 64 * o : 64 * o + 64], jnp.zeros((8, 64), F32)]
@@ -381,22 +382,21 @@
                 settle_y(s)
                 for f in (2, 3):
                     arrive(s, f)
-                more = mm(cx[...], late_h[128:256, :])
                 for f in (0, 1):
-                    at = 56 * f
-                    send[then + f] = send[then + f] + more[at : at + 56, 256 * f : 256 * f + 256]
-                begin(then, then + 1)
-
-            after_x(1)
+                    more = mm(cx[f], late_h[128:256, 256 * f : 256 * f + 256])
+                    send[then + f] = send[then + f] + more[0:56]
+                    begin(then + f)
 
             @pl.when(odd == 0)
             def _():
+                after_x(1)
                 after_x(0)
                 after_y()
 
             @pl.when(odd == 1)
             def _():
                 after_y()
+                after_x(1)
                 after_x(0)
 
         else:
@@ -478,7 +478,7 @@
             pltpu.VMEM((128, 640), BF16),
             pltpu.VMEM((128, 384), BF16),
             pltpu.VMEM((112, 128), BF16),
-            pltpu.VMEM((112, 128), BF16),
+            pltpu.VMEM((2, 64, 128), BF16),
             pltpu.VMEM((4, 64, 64), BF16),
             pltpu.VMEM((4, 64, 256), F32),
             pltpu.VMEM((4, 64, 256), BF16),
@@ -498,7 +498,7 @@
             pltpu.VMEM((128, 256), BF16),
             pltpu.VMEM((12, 56, 256), F32),
             pltpu.VMEM((12, 56, 256), F32),
-            pltpu.SemaphoreType.DMA((1,)),
+            pltpu.SemaphoreType.DMA((2,)),
             pltpu.SemaphoreType.DMA((1,)),
             pltpu.SemaphoreType.DMA((7,)),
         ],

time: 14.7 us -> 14.6 us (level)
  no operation moved by 1% of the time
where the time goes in v6:
time: 14.6 us; the launch traced here: 14.5 us
  Pallas kernels  13.1 us (90%)
  other arithmetic  0.72 us (5%)
  between operations  0.64 us (4%)
    pallas_call x1, Pallas kernels, shards(): pl.pallas_call(kernel, out_shape=(out, out, out), in_specs=[hbm] * 10, ou...  13.1 us
    add x1, other arithmetic, shards(): displacement_out = opened + substep * velocity_out  0.72 us

profile of v6, /device:TPU:1, one launch (start us, length us, event | category | flops | bytes accessed | tf_op | source)
XLA Modules:
  0.0 14.5 jit_solution(12953273811599274901)
XLA Ops:
  0.6 13.1 %shard_map.113 = (f32[240,128]{1,0:T(8,128)S(1)}, f32[240,128]{1,0:T(8,128)S(1)}, f32[240,128]{1,0:T(8,128)S(1)}) custom-call(f32[240,128]{1,0:T(8,128)} %bitcast.11, f32[240,128]{1,0:T(8,128)} %bitcast.12, f32[4,128]{1,0:T(4,128)} %bitcast.15, f32[60,243]{1,0:T(8,128)} %bitcast.14, f32[6,54,60]{2,1,0:T(8,128)} %trace_in.1, f32[6,54,60]{2,1,0:T(8,128)} %bitcast.8, ...), custom_call_target="tpu_custom_call" | custom-call | tf_op jit(solution)/shard_map/pallas_call | solution.py:466
  13.8 0.7 %multiply_add_fusion = (f32[240,128]{1,0:T(8,128)}, f32[240,128]{1,0:T(8,128)}) fusion(f32[240,128]{1,0:T(8,128)S(1)} %get-tuple-element.5, f32[240,128]{1,0:T(8,128)S(1)} %get-tuple-element.6, f32[240,128]{1,0:T(8,128)S(1)} %get-tuple-element.7), kind=kLoop, calls=%fused_computation | loop fusion | flops 122880 | bytes 614400 | tf_op jit(solution)/shard_map/add | solution.py:510

commit v7 on v6

--- a/solution.py
+++ b/solution.py
@@ -193,9 +193,7 @@
     high, low = halves(jnp.concatenate(reach, axis=0)[:, 0:64])
     carry = mm(high, lb_h[:, 0:256]) + mm(low, lb_h[:, 0:256]) + mm(high, lb_hl[64:128, 0:256])
     cy[...] = carry[112:224, 0:128].astype(BF16)
-    for f in range(2):
-        pieces = [carry[56 * f : 56 * f + 56, 128:256], jnp.zeros((8, 128), F32)]
-        cx[f] = jnp.concatenate(pieces, axis=0).astype(BF16)
+    cx[...] = carry[0:112, 128:256].astype(BF16)
     for f in range(4):
         o = f ^ 1
         pieces = [carry[56 * o : 56 * o + 56, 64 * o : 64 * o + 64], jnp.zeros((8, 64), F32)]
@@ -382,21 +380,22 @@
                 settle_y(s)
                 for f in (2, 3):
                     arrive(s, f)
+                more = mm(cx[...], late_h[128:256, :])
                 for f in (0, 1):
-                    more = mm(cx[f], late_h[128:256, 256 * f : 256 * f + 256])
-                    send[then + f] = send[then + f] + more[0:56]
-                    begin(then + f)
+                    at = 56 * f
+                    send[then + f] = send[then + f] + more[at : at + 56, 256 * f : 256 * f + 256]
+                begin(then, then + 1)
+
+            after_x(1)
 
             @pl.when(odd == 0)
             def _():
-                after_x(1)
                 after_x(0)
                 after_y()
 
             @pl.when(odd == 1)
             def _():
                 after_y()
-                after_x(1)
                 after_x(0)
 
         else:
@@ -478,7 +477,7 @@
             pltpu.VMEM((128, 640), BF16),
             pltpu.VMEM((128, 384), BF16),
             pltpu.VMEM((112, 128), BF16),
-            pltpu.VMEM((2, 64, 128), BF16),
+            pltpu.VMEM((112, 128), BF16),
             pltpu.VMEM((4, 64, 64), BF16),
             pltpu.VMEM((4, 64, 256), F32),
             pltpu.VMEM((4, 64, 256), BF16),

time: 14.6 us -> 14.6 us (level)
  no operation moved by 1% of the time
where the time goes in v7:
time: 14.6 us; the launch traced here: 14.5 us
  Pallas kernels  13.1 us (90%)
  other arithmetic  0.72 us (5%)
  between operations  0.64 us (4%)
    pallas_call x1, Pallas kernels, shards(): pl.pallas_call(kernel, out_shape=(out, out, out), in_specs=[hbm] * 10, ou...  13.1 us
    add x1, other arithmetic, shards(): displacement_out = opened + substep * velocity_out  0.72 us

profile of v7, /device:TPU:1, one launch (start us, length us, event | category | flops | bytes accessed | tf_op | source)
XLA Modules:
  0.0 14.5 jit_solution(184852185428542090)
XLA Ops:
  0.6 13.1 %shard_map.113 = (f32[240,128]{1,0:T(8,128)S(1)}, f32[240,128]{1,0:T(8,128)S(1)}, f32[240,128]{1,0:T(8,128)S(1)}) custom-call(f32[240,128]{1,0:T(8,128)} %bitcast.11, f32[240,128]{1,0:T(8,128)} %bitcast.12, f32[4,128]{1,0:T(4,128)} %bitcast.15, f32[60,243]{1,0:T(8,128)} %bitcast.14, f32[6,54,60]{2,1,0:T(8,128)} %trace_in.1, f32[6,54,60]{2,1,0:T(8,128)} %bitcast.8, ...), custom_call_target="tpu_custom_call" | custom-call | tf_op jit(solution)/shard_map/pallas_call | solution.py:465
  13.8 0.7 %multiply_add_fusion = (f32[240,128]{1,0:T(8,128)}, f32[240,128]{1,0:T(8,128)}) fusion(f32[240,128]{1,0:T(8,128)S(1)} %get-tuple-element.5, f32[240,128]{1,0:T(8,128)S(1)} %get-tuple-element.6, f32[240,128]{1,0:T(8,128)S(1)} %get-tuple-element.7), kind=kLoop, calls=%fused_computation | loop fusion | flops 122880 | bytes 614400 | tf_op jit(solution)/shard_map/add | solution.py:509
